TPU v7x, 256 devices: a whole 4x4x8 slice. The times are simulated.
256 devices in a mesh: section: 2 (over y_hi), freq: 64 (over y_lo, x, z), pos: 2 (over core).
Axes of the slice: x: 4, y: 4 (y_hi: 2, y_lo: 2; y = y_hi * 2 + y_lo), z: 8, core: 2. Of those that a mesh axis runs over, the one named last changes fastest.
Arguments:
- raw_capture: bfloat16 [4, 128, 128, 4096], P('pos', ('section', 'freq')), may hold values from -6 to 6
- band_bins: int32 [1024], replicated, may hold values from 64 to 1023
- probe_index: int32 [4], P('pos'), may hold values from 0 to 63
Outputs:
- panel_image: float32 [4, 512], P(None, ('section', 'freq'))
All inputs are finite; a program needn't handle non-finite values.
Results may differ from a plain program's by a relative error of at most 0.0058.
Values may be sent and summed in bfloat16 or wider, within the bound.
A program may use at most 64 MiB of HBM per device.

v0:
```python
import math

import jax
import jax.numpy as jnp
from jax import lax
from jax.sharding import PartitionSpec as P

IX = 512
IZ = 4


wave_speed = 0.5
pixel_pitch = 0.25
depth_start = 20.0
probe_anchor = 32.0


def time_table(band_bins, samples):
    sample_ids = jnp.arange(samples, dtype=jnp.int32)
    phase_turns = sample_ids[:, None] * band_bins[None, :] % samples
    phase_value = phase_turns.astype(jnp.float32) * (2.0 * math.pi / samples)
    return jnp.concatenate([jnp.cos(phase_value), -jnp.sin(phase_value)], axis=1).astype(
        jnp.bfloat16
    )


def element_table(elems):
    element_pos = jnp.arange(elems, dtype=jnp.float32) - (elems - 1) / 2.0
    wavenumber = (jnp.arange(elems, dtype=jnp.float32) - elems // 2) * (2.0 * math.pi / elems)
    phase_angle = element_pos[:, None] * wavenumber[None, :]
    cosine = jnp.cos(phase_angle)
    sine_part = jnp.sin(phase_angle)
    upper_rows = jnp.concatenate([cosine, -sine_part], axis=1)
    lower_rows = jnp.concatenate([sine_part, cosine], axis=1)
    return jnp.concatenate([upper_rows, lower_rows], axis=0).astype(jnp.bfloat16)


def focus_bin(spectrum, bin_value, index_value, tx_coord, samples):
    elems = spectrum.shape[1] // 2
    across = jnp.tile(jnp.arange(IX, dtype=jnp.float32) * pixel_pitch, IZ)
    depth_rows = jnp.repeat(depth_start + jnp.arange(IZ, dtype=jnp.float32) * pixel_pitch, IX)
    centre = probe_anchor + index_value.astype(jnp.float32)
    wave_number = bin_value.astype(jnp.float32) * (2.0 * math.pi / samples) / wave_speed
    lateral = across - centre
    offset = lateral[None, :] - tx_coord[:, None]
    distance = jnp.sqrt(offset * offset + depth_rows[None, :] * depth_rows[None, :])
    send_phase = wave_number * distance
    wavenumber = (jnp.arange(elems, dtype=jnp.float32) - elems // 2) * (2.0 * math.pi / elems)
    vertical = jnp.sqrt(jnp.maximum(wave_number * wave_number - wavenumber * wavenumber, 0.0))
    weight = vertical / wave_number
    recv_phase = wavenumber[:, None] * lateral[None, :] + vertical[:, None] * depth_rows[None, :]
    recv_real = weight[:, None] * jnp.cos(recv_phase)
    recv_imag = weight[:, None] * jnp.sin(recv_phase)
    recv_table = jnp.concatenate(
        [
            jnp.concatenate([recv_real, recv_imag], axis=1),
            jnp.concatenate([-recv_imag, recv_real], axis=1),
        ],
        axis=0,
    ).astype(jnp.bfloat16)
    field_sum = jnp.dot(spectrum, recv_table, preferred_element_type=jnp.float32)
    pixels = across.shape[0]
    return jnp.sum(
        jnp.cos(send_phase) * field_sum[:, :pixels] - jnp.sin(send_phase) * field_sum[:, pixels:],
        axis=0,
    )


def per_device(raw_capture, band_bins, probe_index):
    pos_here, tx_here, elems, samples = raw_capture.shape
    bins_all = band_bins.shape[0]
    groups = lax.axis_size(("section", "freq"))
    slab_width = bins_all // groups
    sample_rows = raw_capture.reshape(pos_here * tx_here * elems, samples)
    element_dft = element_table(elems).reshape(2, elems, 2 * elems)
    block_size = min(bins_all, 256)
    wave_blocks = []
    for block_start in range(0, bins_all, block_size):
        dft_table = time_table(band_bins[block_start : block_start + block_size], samples)
        spectrum = jnp.dot(sample_rows, dft_table, preferred_element_type=jnp.float32).astype(
            jnp.bfloat16
        )
        spectrum = spectrum.reshape(pos_here, tx_here, elems, 2, block_size)
        wave_rows = jnp.einsum(
            "ptrcb,crm->bptm", spectrum, element_dft, preferred_element_type=jnp.float32
        )
        wave_blocks.append(wave_rows.astype(jnp.bfloat16))
    wavefield = jnp.concatenate(wave_blocks, axis=0)
    slab_data = lax.all_to_all(
        wavefield, ("section", "freq"), split_axis=0, concat_axis=2, tiled=True
    )
    tx_coord = jnp.arange(elems, dtype=jnp.float32) - (elems - 1) / 2.0
    slab_index = lax.axis_index(("section", "freq"))
    local_bins = lax.dynamic_slice_in_dim(band_bins, slab_index * slab_width, slab_width)

    def add_bin(bin_step, image_sum):
        bin_value = lax.dynamic_index_in_dim(local_bins, bin_step, keepdims=False)
        bin_slab = lax.dynamic_index_in_dim(slab_data, bin_step, keepdims=False)
        for member in range(pos_here):
            image_sum = image_sum + focus_bin(
                bin_slab[member], bin_value, probe_index[member], tx_coord, samples
            )
        return image_sum

    image_sum = lax.fori_loop(0, slab_width, add_bin, jnp.zeros((IZ * IX,), jnp.float32))
    positions_all = pos_here * lax.axis_size("pos")
    image_scale = 1.0 / math.sqrt(float(samples * elems**3 * bins_all * positions_all))
    partial_image = (image_sum * image_scale).reshape(IZ, IX)
    panel_sum = lax.psum(partial_image, "pos")
    return lax.psum_scatter(panel_sum, ("section", "freq"), scatter_dimension=1, tiled=True)


def solution(mesh):
    in_specs = (P("pos", ("section", "freq"), None, None), P(), P("pos"))
    out_specs = P(None, ("section", "freq"))
    return jax.shard_map(
        per_device, mesh=mesh, in_specs=in_specs, out_specs=out_specs, check_vma=False
    )
```

profile of v0, /device:TPU:1, one launch (start us, length us, event | category | flops | bytes accessed | tf_op | source)
XLA Modules:
  0.0 664.7 jit_solution(12459725606110125131)
XLA Ops:
  0.0 0.9 fusion.116
  0.9 34.8 %cosine_convert_fusion.2 = (bf16[4096,256]{1,0:T(8,128)(2,1)S(1)}, bf16[4096,256]{1,0:T(8,128)(2,1)S(1)}, bf16[4096,256]{1,0:T(8,128)(2,1)}, bf16[4096,256]{1,0:T(8,128)(2,1)}) fusion(s32[256]{0:T(256)S(1)} %get-tuple-element.294, s32[256]{0:T(256)S(1)} %get-tuple-element.293), kind=kLoop, calls=%fused_computation.103 | loop fusion | flops 35651584 | bytes 8390656 | tf_op jit(solution)/shard_map/convert.16
  35.7 1.3 fusion.95
  37.1 3.5 fusion.92
  40.7 0.3 fusion.110
  41.0 0.2 fusion.90
  41.3 0.2 fusion.91
  41.5 34.8 %cosine_convert_fusion = (bf16[4096,256]{1,0:T(8,128)(2,1)}, bf16[4096,256]{1,0:T(8,128)(2,1)}, bf16[4096,256]{1,0:T(8,128)(2,1)S(1)}, bf16[4096,256]{1,0:T(8,128)(2,1)S(1)}) fusion(s32[256]{0:T(256)S(1)} %get-tuple-element.295, s32[256]{0:T(256)S(1)} %get-tuple-element.296), kind=kLoop, calls=%fused_computation.95 | loop fusion | flops 35651584 | bytes 8390656 | tf_op jit(solution)/shard_map/convert.12
  76.3 1.3 fusion.98
  77.7 0.2 fusion.89
  77.9 3.5 fusion.101
  81.5 0.2 fusion.88
  81.7 0.1 pad_maximum_fusion
  81.8 2.1 copy.13
  83.9 16.3 %all-to-all-start = ((bf16[1024,2,1,256]{3,1,2,0:T(2,128)(2,1)}), bf16[1024,2,1,256]{3,1,2,0:T(2,128)(2,1)S(1)}, u32[]{:S(2)}, u32[]{:S(2)}) async-start(bf16[1024,2,1,256]{3,1,2,0:T(2,128)(2,1)} %copy.13), calls=%async_computation | async-start | bytes 2097152 | tf_op jit(solution)/shard_map/all_to_all | solution.py:89
  100.3 0.8 dynamic_slice.31
  101.0 0.6 fusion.117
  102.9 0.6 dynamic-slice
  104.2 26.3 %all-to-all-done = bf16[1024,2,1,256]{3,1,2,0:T(2,128)(2,1)S(1)} async-done(((bf16[1024,2,1,256]{3,1,2,0:T(2,128)(2,1)}), bf16[1024,2,1,256]{3,1,2,0:T(2,128)(2,1)S(1)}, u32[]{:S(2)}, u32[]{:S(2)}) %all-to-all-start) | async-done | bytes 1048608 | tf_op jit(solution)/shard_map/all_to_all | solution.py:89
  130.5 1.3 copy.32
  131.8 180.7 %while.19 = (s32[]{:T(128)}, f32[2048]{0:T(1024)S(1)}, s32[8]{0:T(128)S(1)}, f32[]{:T(128)}, bf16[8,2,128,256]{3,2,1,0:T(8,128)(2,1)}, /*index=5*/f32[]{:T(128)}...) while((s32[]{:T(128)}, f32[2048]{0:T(1024)S(1)}, s32[8]{0:T(128)S(1)}, ...), condition=%wide.region_3.4_spmd.clone.clone, body=%wide.region_0.3_spmd.clone.clone.sunk | while | flops 562305664 | bytes 17118476 | solution.py:105
  131.8 0.6 dynamic_slice.37
  133.2 8.9 %fusion.137 = (bf16[128,2048]{1,0:T(8,128)(2,1)}, bf16[128,2048]{1,0:T(8,128)(2,1)}, bf16[128,2048]{1,0:T(8,128)(2,1)}, bf16[128,2048]{1,0:T(8,128)(2,1)S(1)}, b...) fusion(f32[2048]{0:T(1024)S(1)} %bitcast.132, f32[2048]{0:T(1024)S(1)} %bitcast.125, ...), kind=kLoop, calls=%fused_computation.30.clone.1 | loop fusion | flops 4456448 | bytes 3171840 | tf_op jit(solution)/shard_map/convert.5
  142.1 2.1 fusion.139
  144.2 1.3 fusion.138
  145.5 8.8 %fusion.140 = (f32[2048]{0:T(1024)S(1)}, f32[2048]{0:T(1024)S(1)}) fusion(f32[128,4096]{1,0:T(8,128)S(1)} %fusion.138, f32[2048]{0:T(1024)S(1)} %mul.1013, f32[128]{0:T(128)S(1)} %iota_add_fusion.3, f32[2048]{0:T(1024)S(1)} %bitcast.135, f32[]{:T(128)} %bitcast.118, f32[128,4096]{1,0:T(8,128)S(1)} %fusion.139, f32[2048]{0:T(1024)S(1)} %bitcast.133), kind=kLoop, calls=%fused_computation.25.clone.1 | loop fusion | flops 4190208 | bytes 4235780 | tf_op jit(solution)/shard_map/while/body/eval_jaxpr/reduce_sum | solution.py:63
  154.4 0.6 dynamic_slice.37
  155.8 8.9 %fusion.137 = (bf16[128,2048]{1,0:T(8,128)(2,1)}, bf16[128,2048]{1,0:T(8,128)(2,1)}, bf16[128,2048]{1,0:T(8,128)(2,1)}, bf16[128,2048]{1,0:T(8,128)(2,1)S(1)}, b...) fusion(f32[2048]{0:T(1024)S(1)} %bitcast.132, f32[2048]{0:T(1024)S(1)} %bitcast.125, ...), kind=kLoop, calls=%fused_computation.30.clone.1 | loop fusion | flops 4456448 | bytes 3171840 | tf_op jit(solution)/shard_map/convert.5
  164.7 2.1 fusion.139
  166.8 1.3 fusion.138
  168.1 8.8 %fusion.140 = (f32[2048]{0:T(1024)S(1)}, f32[2048]{0:T(1024)S(1)}) fusion(f32[128,4096]{1,0:T(8,128)S(1)} %fusion.138, f32[2048]{0:T(1024)S(1)} %mul.1013, f32[128]{0:T(128)S(1)} %iota_add_fusion.3, f32[2048]{0:T(1024)S(1)} %bitcast.135, f32[]{:T(128)} %bitcast.118, f32[128,4096]{1,0:T(8,128)S(1)} %fusion.139, f32[2048]{0:T(1024)S(1)} %bitcast.133), kind=kLoop, calls=%fused_computation.25.clone.1 | loop fusion | flops 4190208 | bytes 4235780 | tf_op jit(solution)/shard_map/while/body/eval_jaxpr/reduce_sum | solution.py:63
  176.9 0.6 dynamic_slice.37
  178.4 8.9 %fusion.137 = (bf16[128,2048]{1,0:T(8,128)(2,1)}, bf16[128,2048]{1,0:T(8,128)(2,1)}, bf16[128,2048]{1,0:T(8,128)(2,1)}, bf16[128,2048]{1,0:T(8,128)(2,1)S(1)}, b...) fusion(f32[2048]{0:T(1024)S(1)} %bitcast.132, f32[2048]{0:T(1024)S(1)} %bitcast.125, ...), kind=kLoop, calls=%fused_computation.30.clone.1 | loop fusion | flops 4456448 | bytes 3171840 | tf_op jit(solution)/shard_map/convert.5
  187.3 2.1 fusion.139
  189.4 1.3 fusion.138
  190.7 8.8 %fusion.140 = (f32[2048]{0:T(1024)S(1)}, f32[2048]{0:T(1024)S(1)}) fusion(f32[128,4096]{1,0:T(8,128)S(1)} %fusion.138, f32[2048]{0:T(1024)S(1)} %mul.1013, f32[128]{0:T(128)S(1)} %iota_add_fusion.3, f32[2048]{0:T(1024)S(1)} %bitcast.135, f32[]{:T(128)} %bitcast.118, f32[128,4096]{1,0:T(8,128)S(1)} %fusion.139, f32[2048]{0:T(1024)S(1)} %bitcast.133), kind=kLoop, calls=%fused_computation.25.clone.1 | loop fusion | flops 4190208 | bytes 4235780 | tf_op jit(solution)/shard_map/while/body/eval_jaxpr/reduce_sum | solution.py:63
  199.5 0.6 dynamic_slice.37
  201.0 8.9 %fusion.137 = (bf16[128,2048]{1,0:T(8,128)(2,1)}, bf16[128,2048]{1,0:T(8,128)(2,1)}, bf16[128,2048]{1,0:T(8,128)(2,1)}, bf16[128,2048]{1,0:T(8,128)(2,1)S(1)}, b...) fusion(f32[2048]{0:T(1024)S(1)} %bitcast.132, f32[2048]{0:T(1024)S(1)} %bitcast.125, ...), kind=kLoop, calls=%fused_computation.30.clone.1 | loop fusion | flops 4456448 | bytes 3171840 | tf_op jit(solution)/shard_map/convert.5
  209.9 2.1 fusion.139
  211.9 1.3 fusion.138
  213.3 8.8 %fusion.140 = (f32[2048]{0:T(1024)S(1)}, f32[2048]{0:T(1024)S(1)}) fusion(f32[128,4096]{1,0:T(8,128)S(1)} %fusion.138, f32[2048]{0:T(1024)S(1)} %mul.1013, f32[128]{0:T(128)S(1)} %iota_add_fusion.3, f32[2048]{0:T(1024)S(1)} %bitcast.135, f32[]{:T(128)} %bitcast.118, f32[128,4096]{1,0:T(8,128)S(1)} %fusion.139, f32[2048]{0:T(1024)S(1)} %bitcast.133), kind=kLoop, calls=%fused_computation.25.clone.1 | loop fusion | flops 4190208 | bytes 4235780 | tf_op jit(solution)/shard_map/while/body/eval_jaxpr/reduce_sum | solution.py:63
  222.1 0.6 dynamic_slice.37
  223.6 8.9 %fusion.137 = (bf16[128,2048]{1,0:T(8,128)(2,1)}, bf16[128,2048]{1,0:T(8,128)(2,1)}, bf16[128,2048]{1,0:T(8,128)(2,1)}, bf16[128,2048]{1,0:T(8,128)(2,1)S(1)}, b...) fusion(f32[2048]{0:T(1024)S(1)} %bitcast.132, f32[2048]{0:T(1024)S(1)} %bitcast.125, ...), kind=kLoop, calls=%fused_computation.30.clone.1 | loop fusion | flops 4456448 | bytes 3171840 | tf_op jit(solution)/shard_map/convert.5
  232.5 2.1 fusion.139
  234.5 1.3 fusion.138
  235.9 8.8 %fusion.140 = (f32[2048]{0:T(1024)S(1)}, f32[2048]{0:T(1024)S(1)}) fusion(f32[128,4096]{1,0:T(8,128)S(1)} %fusion.138, f32[2048]{0:T(1024)S(1)} %mul.1013, f32[128]{0:T(128)S(1)} %iota_add_fusion.3, f32[2048]{0:T(1024)S(1)} %bitcast.135, f32[]{:T(128)} %bitcast.118, f32[128,4096]{1,0:T(8,128)S(1)} %fusion.139, f32[2048]{0:T(1024)S(1)} %bitcast.133), kind=kLoop, calls=%fused_computation.25.clone.1 | loop fusion | flops 4190208 | bytes 4235780 | tf_op jit(solution)/shard_map/while/body/eval_jaxpr/reduce_sum | solution.py:63
  244.7 0.6 dynamic_slice.37
  246.2 8.9 %fusion.137 = (bf16[128,2048]{1,0:T(8,128)(2,1)}, bf16[128,2048]{1,0:T(8,128)(2,1)}, bf16[128,2048]{1,0:T(8,128)(2,1)}, bf16[128,2048]{1,0:T(8,128)(2,1)S(1)}, b...) fusion(f32[2048]{0:T(1024)S(1)} %bitcast.132, f32[2048]{0:T(1024)S(1)} %bitcast.125, ...), kind=kLoop, calls=%fused_computation.30.clone.1 | loop fusion | flops 4456448 | bytes 3171840 | tf_op jit(solution)/shard_map/convert.5
  255.0 2.1 fusion.139
  257.1 1.3 fusion.138
  258.4 8.8 %fusion.140 = (f32[2048]{0:T(1024)S(1)}, f32[2048]{0:T(1024)S(1)}) fusion(f32[128,4096]{1,0:T(8,128)S(1)} %fusion.138, f32[2048]{0:T(1024)S(1)} %mul.1013, f32[128]{0:T(128)S(1)} %iota_add_fusion.3, f32[2048]{0:T(1024)S(1)} %bitcast.135, f32[]{:T(128)} %bitcast.118, f32[128,4096]{1,0:T(8,128)S(1)} %fusion.139, f32[2048]{0:T(1024)S(1)} %bitcast.133), kind=kLoop, calls=%fused_computation.25.clone.1 | loop fusion | flops 4190208 | bytes 4235780 | tf_op jit(solution)/shard_map/while/body/eval_jaxpr/reduce_sum | solution.py:63
  267.3 0.6 dynamic_slice.37
  268.7 8.9 %fusion.137 = (bf16[128,2048]{1,0:T(8,128)(2,1)}, bf16[128,2048]{1,0:T(8,128)(2,1)}, bf16[128,2048]{1,0:T(8,128)(2,1)}, bf16[128,2048]{1,0:T(8,128)(2,1)S(1)}, b...) fusion(f32[2048]{0:T(1024)S(1)} %bitcast.132, f32[2048]{0:T(1024)S(1)} %bitcast.125, ...), kind=kLoop, calls=%fused_computation.30.clone.1 | loop fusion | flops 4456448 | bytes 3171840 | tf_op jit(solution)/shard_map/convert.5
  277.6 2.1 fusion.139
  279.7 1.3 fusion.138
  281.0 8.8 %fusion.140 = (f32[2048]{0:T(1024)S(1)}, f32[2048]{0:T(1024)S(1)}) fusion(f32[128,4096]{1,0:T(8,128)S(1)} %fusion.138, f32[2048]{0:T(1024)S(1)} %mul.1013, f32[128]{0:T(128)S(1)} %iota_add_fusion.3, f32[2048]{0:T(1024)S(1)} %bitcast.135, f32[]{:T(128)} %bitcast.118, f32[128,4096]{1,0:T(8,128)S(1)} %fusion.139, f32[2048]{0:T(1024)S(1)} %bitcast.133), kind=kLoop, calls=%fused_computation.25.clone.1 | loop fusion | flops 4190208 | bytes 4235780 | tf_op jit(solution)/shard_map/while/body/eval_jaxpr/reduce_sum | solution.py:63
  289.9 0.6 dynamic_slice.37
  291.3 8.9 %fusion.137 = (bf16[128,2048]{1,0:T(8,128)(2,1)}, bf16[128,2048]{1,0:T(8,128)(2,1)}, bf16[128,2048]{1,0:T(8,128)(2,1)}, bf16[128,2048]{1,0:T(8,128)(2,1)S(1)}, b...) fusion(f32[2048]{0:T(1024)S(1)} %bitcast.132, f32[2048]{0:T(1024)S(1)} %bitcast.125, ...), kind=kLoop, calls=%fused_computation.30.clone.1 | loop fusion | flops 4456448 | bytes 3171840 | tf_op jit(solution)/shard_map/convert.5
  300.2 2.1 fusion.139
  302.3 1.3 fusion.138
  303.6 8.8 %fusion.140 = (f32[2048]{0:T(1024)S(1)}, f32[2048]{0:T(1024)S(1)}) fusion(f32[128,4096]{1,0:T(8,128)S(1)} %fusion.138, f32[2048]{0:T(1024)S(1)} %mul.1013, f32[128]{0:T(128)S(1)} %iota_add_fusion.3, f32[2048]{0:T(1024)S(1)} %bitcast.135, f32[]{:T(128)} %bitcast.118, f32[128,4096]{1,0:T(8,128)S(1)} %fusion.139, f32[2048]{0:T(1024)S(1)} %bitcast.133), kind=kLoop, calls=%fused_computation.25.clone.1 | loop fusion | flops 4190208 | bytes 4235780 | tf_op jit(solution)/shard_map/while/body/eval_jaxpr/reduce_sum | solution.py:63
  312.5 292.0 %all-reduce = f32[4,512]{1,0:T(4,128)S(1)} all-reduce(f32[4,512]{1,0:T(4,128)S(1)} %reshape.147), channel_id=2, replica_groups=mesh['section'=2,'freq'=64,'pos'=2] {'section','freq'}, use_global_device_ids=true, to_apply=%region_5.6.clone | all-reduce | flops 2048 | bytes 16384
  604.5 0.1 constant_dynamic-slice_fusion
  604.6 60.1 %psum.8 = f32[4,4]{1,0:T(4,128)} all-reduce(f32[4,4]{1,0:T(4,128)S(1)} %constant_dynamic-slice_fusion), channel_id=1, replica_groups=mesh['section'=2,'freq'=64,'pos'=2] {'pos'}, use_global_device_ids=true, to_apply=%region_4.5 | all-reduce | flops 16 | bytes 128 | tf_op jit(solution)/shard_map/psum | solution.py:109
  (135 shorter events, 1.6 us)
Async XLA Ops:
  0.0 35.7 %copy-start = (bf16[2,1,128,4096]{3,2,1,0:T(8,128)(2,1)S(1)}, bf16[2,1,128,4096]{3,2,1,0:T(8,128)(2,1)}, u32[]{:S(2)}) copy-start(bf16[2,1,128,4096]{3,2,1,0:T(8,128)(2,1)} %param.5) | copy-start | bytes 6291460
  81.8 19.2 %copy-start.2 = (s32[2]{0:T(128)S(1)}, s32[2]{0:T(128)}, u32[]{:S(2)}) copy-start(s32[2]{0:T(128)} %param.7) | copy-start | bytes 28
  81.8 21.1 %copy-start.3 = (u32[256]{0:T(256)S(1)}, u32[256]{0:T(256)}, u32[]{:S(2)}) copy-start(u32[256]{0:T(256)} %constant.200) | copy-start | bytes 3076
  83.9 46.6 %all-to-all-start = ((bf16[1024,2,1,256]{3,1,2,0:T(2,128)(2,1)}), bf16[1024,2,1,256]{3,1,2,0:T(2,128)(2,1)S(1)}, u32[]{:S(2)}, u32[]{:S(2)}) async-start(bf16[1024,2,1,256]{3,1,2,0:T(2,128)(2,1)} %copy.13), calls=%async_computation | async-start | bytes 2097152 | tf_op jit(solution)/shard_map/all_to_all | solution.py:89
  142.1 2.1 copy-start.1
  164.7 2.1 copy-start.1
  187.3 2.1 copy-start.1
  209.9 2.1 copy-start.1
  232.5 2.1 copy-start.1
  255.0 2.1 copy-start.1
  277.6 2.1 copy-start.1
  300.2 2.1 copy-start.1
where the time goes:
time: 666 us; the launch traced here: 665 us
  blocking collectives  352 us (53%)
  other arithmetic  212 us (32%)
  matrix products  37.3 us (6%)
  waiting for transfers between devices  26.3 us (4%)
  starting transfers between devices  16.3 us (2%)
  local copies, waits for them, and re-layouts  12.6 us (2%)
    unnamed x1, blocking collectives  292 us
    another operation x11, other arithmetic  141 us
    reduce_sum x8, other arithmetic, focus_bin(): jnp.sum(jnp.cos(send_phase) * field_sum[:, :pixels] - jnp.sin(send_phase)...  70.4 us
    psum x1, blocking collectives, per_device(): panel_sum = lax.psum(partial_image, 'pos')  60.1 us
    dot_general x16, matrix products, focus_bin(): jnp.dot(spectrum, recv_table, preferred_element_type=jnp.float32)  26.8 us
    all_to_all x1, waiting for transfers between devices, per_device(): lax.all_to_all(wavefield, ('section', 'freq'), split_axis=0, concat_axis=...  26.3 us
    all_to_all x1, starting transfers between devices, per_device(): lax.all_to_all(wavefield, ('section', 'freq'), split_axis=0, concat_axis=...  16.3 us
  transfers between devices with their start and end apart: 1, of which 1 were waited for; matrix products, arithmetic and copies ran while one was open for 0% of the time, Pallas kernels for 0%

commit v1 on v0

v1 whole, which is shorter than its diff:
```python
import functools
import math

import jax
import jax.numpy as jnp
import ml_dtypes
import numpy as np
from jax import lax
from jax.experimental import pallas as pl
from jax.experimental.pallas import tpu as pltpu
from jax.sharding import PartitionSpec as P

NE = 128
NT = 4096
NF = 1024
IX = 512
IZ = 4
POS_HERE = 2
RADIX = 16
QUARTER = NT // 4
CENTRES = 64

wave_speed = 0.5
pixel_pitch = 0.25
depth_start = 20.0
probe_anchor = 32.0

EVEN = ((0, 8, 4, -4), (2, -2, 6, -6))
ODD = ((1, 5, -3, -7), (3, 7, -1, -5))


def group_of(offset):
    if offset in (0, 8):
        return 7, 8 * offset
    return abs(offset) - 1, 0 if offset > 0 else CENTRES


def time_tables():
    samples = np.arange(QUARTER)
    centres = RADIX * (np.arange(CENTRES) + 1)

    def parts(offsets):
        bins = np.concatenate([centres + offset for offset in offsets])
        angle = 2.0 * np.pi * (bins[:, None] * samples[None, :] % NT) / NT
        return np.cos(angle), -np.sin(angle)

    even = np.stack([np.concatenate(parts(offsets), axis=0) for offsets in EVEN])
    re1, im1 = parts(ODD[0])
    re3, im3 = parts(ODD[1])
    odd = np.concatenate(
        [np.concatenate([re1, im1], axis=1), np.concatenate([im3, re3], axis=1)], axis=0
    )
    return even.astype(ml_dtypes.bfloat16), odd.astype(ml_dtypes.bfloat16)


def element_table():
    pos = np.arange(NE) - (NE - 1) / 2.0
    angle = pos[:, None] * (np.arange(NE) - NE // 2)[None, :] * (2.0 * np.pi / NE)
    c, s = np.cos(angle), np.sin(angle)
    table = np.concatenate([np.concatenate([c, -s], axis=1), np.concatenate([s, c], axis=1)], axis=0)
    return table.astype(ml_dtypes.bfloat16)


def column_table():
    order = np.arange(NE) - NE // 2
    angle = 2.0 * np.pi * (order[:, None] * np.arange(IX)[None, :] % IX) / IX
    cosine, sine = np.cos(angle), np.sin(angle)
    tiles = []
    for start in range(0, IX, 128):
        c, s = cosine[:, start : start + 128], sine[:, start : start + 128]
        tiles.append(
            np.concatenate([np.concatenate([c, s], axis=1), np.concatenate([-s, c], axis=1)], axis=0)
        )
    return np.stack(tiles).astype(ml_dtypes.bfloat16)


def depth_table():
    centres = RADIX * (np.arange(CENTRES) + 1)
    wavenumber = (np.arange(NE) - NE // 2) * (2.0 * np.pi / NE)

    def parts(offset):
        k = (centres + offset)[:, None] * (2.0 * np.pi / NT) / wave_speed
        vertical = np.sqrt(np.maximum(k * k - wavenumber[None, :] ** 2, 0.0))
        weight = vertical / k
        first = weight * np.exp(1j * vertical * depth_start)
        step = np.exp(1j * vertical * pixel_pitch)
        return np.stack([first.real, first.imag, step.real, step.imag])

    groups = [np.concatenate([parts(offset), parts(-offset)], axis=1) for offset in range(1, 8)]
    groups.append(np.concatenate([parts(0), parts(8)], axis=1))
    return np.stack(groups, axis=1).astype(np.float32)


def turn_pair(turns):
    x = turns - jnp.floor(turns + 0.5)
    square = x * x
    sine = jnp.full_like(x, math.pi**13 / math.factorial(13))
    for power in (11, 9, 7, 5, 3, 1):
        sign = 1.0 if power % 4 == 1 else -1.0
        sine = sine * square + sign * math.pi**power / math.factorial(power)
    sine = sine * x
    cosine = jnp.full_like(x, math.pi**12 / math.factorial(12))
    for power in (10, 8, 6, 4, 2, 0):
        sign = 1.0 if power % 4 == 0 else -1.0
        cosine = cosine * square + sign * math.pi**power / math.factorial(power)
    return 1.0 - 2.0 * sine * sine, 2.0 * sine * cosine


def transposed_dot(a, b):
    return lax.dot_general(a, b, (((1,), (1,)), ((), ())), preferred_element_type=jnp.float32)


def focus_kernel(
    probe_ref, tx_ref, bins_ref, raw_ref, even_ref, odd_ref, element_ref, column_ref, depth_ref,
    out_ref, negative, spectra, rows, counts, near, far, image,
):
    bins = bins_ref[...]
    centre = (bins - 9) >> 4
    offset = bins - 16 * centre - 16
    is_centre = jnp.where(lax.broadcasted_iota(jnp.int32, (CENTRES, NF), 0) == centre, 1.0, 0.0)
    is_offset = jnp.where(lax.broadcasted_iota(jnp.int32, (16, NF), 0) - 7 == offset, 1.0, 0.0)
    counts[...] = transposed_dot(is_centre.astype(jnp.bfloat16), is_offset.astype(jnp.bfloat16))

    sub = lax.broadcasted_iota(jnp.int32, (8, 128), 0).astype(jnp.float32) + 1.0
    lane = lax.broadcasted_iota(jnp.int32, (8, 128), 1)
    for p in range(POS_HERE):
        shift = 4 * (probe_ref[p] + int(probe_anchor))
        middle = probe_anchor + probe_ref[p].astype(jnp.float32)
        for tile in range(IX // 128):
            column = ((lane + (128 * tile + shift)) & (IX - 1)).astype(jnp.float32)
            x = (pixel_pitch * column - middle) - tx_ref[0]
            for k in range(IZ):
                z = depth_start + pixel_pitch * k
                turns = jnp.sqrt(x * x + z * z) * (1.0 / (NT * wave_speed))
                c, s = turn_pair(turns * sub)
                near[tile, p * IZ + k, 0], near[tile, p * IZ + k, 1] = c, s
                c, s = turn_pair(turns * (sub * RADIX))
                far[tile, p * IZ + k, 0], far[tile, p * IZ + k, 1] = c, s

    negative[...] = -raw_ref[...]

    def quarters(signs):
        return jnp.concatenate(
            [
                (raw_ref if sign > 0 else negative)[:, q * QUARTER : (q + 1) * QUARTER]
                for q, sign in enumerate(signs)
            ],
            axis=1,
        )

    def keep(values, offsets, part):
        for index, offset in enumerate(offsets):
            group, row = group_of(offset)
            for p in range(POS_HERE):
                spectra[p, group, row : row + CENTRES, part * NE : (part + 1) * NE] = values[
                    index * CENTRES : (index + 1) * CENTRES, p * NE : (p + 1) * NE
                ]

    for index, signs in enumerate(((1, 1, 1, 1), (1, -1, 1, -1))):
        table = even_ref[index]
        out = transposed_dot(jnp.concatenate([table] * 4, axis=1), quarters(signs)).astype(jnp.bfloat16)
        keep(out[: 4 * CENTRES], EVEN[index], 0)
        keep(out[4 * CENTRES :], EVEN[index], 1)
    left, right = odd_ref[:, :QUARTER], odd_ref[:, QUARTER:]
    out = transposed_dot(
        jnp.concatenate([left, right, left, right], axis=1), quarters((1, 1, -1, -1))
    ).astype(jnp.bfloat16)
    keep(out[: 4 * CENTRES], ODD[0], 0)
    keep(out[4 * CENTRES :], ODD[1], 1)
    out = transposed_dot(
        jnp.concatenate([right, left, right, left], axis=1), quarters((1, -1, -1, 1))
    ).astype(jnp.bfloat16)
    keep(out[: 4 * CENTRES], ODD[0], 1)
    keep(out[4 * CENTRES :], ODD[1], 0)

    for group in range(8):
        scales = [
            counts[:, 7 + o : 8 + o] for o in ((group + 1, -group - 1) if group < 7 else (0, 8))
        ]
        for p in range(POS_HERE):
            field = jnp.dot(spectra[p, group], element_ref[...], preferred_element_type=jnp.float32)
            field = field.astype(jnp.bfloat16)
            for block in range(0, CENTRES, 16):
                parts = []
                for half in range(2):
                    at = slice(half * CENTRES + block, half * CENTRES + block + 16)
                    scale = scales[half][block : block + 16]
                    re = field[at, :NE].astype(jnp.float32) * scale
                    im = field[at, NE:].astype(jnp.float32) * scale
                    cosine, sine = depth_ref[0, group, at, :], depth_ref[1, group, at, :]
                    parts.append([re * cosine - im * sine, re * sine + im * cosine])
                for k in range(IZ):
                    if k > 0:
                        for half in range(2):
                            at = slice(half * CENTRES + block, half * CENTRES + block + 16)
                            cosine, sine = depth_ref[2, group, at, :], depth_ref[3, group, at, :]
                            re, im = parts[half]
                            parts[half] = [re * cosine - im * sine, re * sine + im * cosine]
                    (re, im), (re_low, im_low) = parts
                    if group < 7:
                        values = (re + re_low, im + im_low, re - re_low, im - im_low)
                    else:
                        values = (re, im, re_low, im_low)
                    re, im, re_low, im_low = [value.astype(jnp.bfloat16) for value in values]
                    top = slice(block, block + 16)
                    low = slice(CENTRES + block, CENTRES + block + 16)
                    rows[p * IZ + k, group, top, :NE] = re
                    rows[p * IZ + k, group, top, NE:] = im
                    rows[p * IZ + k, group, low, :NE] = re_low
                    rows[p * IZ + k, group, low, NE:] = im_low

    @pl.loop(0, IX // 128)
    def _(tile):
        weights = column_ref[tile]
        for pk in range(POS_HERE * IZ):
            total_re = jnp.zeros((CENTRES, 128), jnp.float32)
            total_im = jnp.zeros((CENTRES, 128), jnp.float32)
            for group in range(8):
                both = jnp.dot(rows[pk, group], weights, preferred_element_type=jnp.float32)
                c, s = near[tile, pk, 0, group : group + 1, :], near[tile, pk, 1, group : group + 1, :]
                low_re, low_im = both[CENTRES:, :128], both[CENTRES:, 128:]
                if group < 7:
                    total_re += c * both[:CENTRES, :128] - s * low_im
                    total_im += c * both[:CENTRES, 128:] + s * low_re
                else:
                    total_re += both[:CENTRES, :128] + (c * low_re - s * low_im)
                    total_im += both[:CENTRES, 128:] + (c * low_im + s * low_re)
            jump_cos = jnp.broadcast_to(far[tile, pk, 0, 7:8, :], (8, 128))
            jump_sin = jnp.broadcast_to(far[tile, pk, 1, 7:8, :], (8, 128))
            re, im = total_re[56:], total_im[56:]
            for g in range(6, -1, -1):
                re, im = (
                    re * jump_cos - im * jump_sin + total_re[8 * g : 8 * g + 8],
                    re * jump_sin + im * jump_cos + total_im[8 * g : 8 * g + 8],
                )
            value = re * far[tile, pk, 0] - im * far[tile, pk, 1]
            image[tile, pk : pk + 1, :] = jnp.sum(value, axis=0, keepdims=True)

    scale = 1.0 / math.sqrt(float(NT * NE**3 * NF * 4))
    both = jnp.concatenate([image[tile] for tile in range(IX // 128)], axis=1)
    shifts = [4 * (probe_ref[p] + int(probe_anchor)) for p in range(POS_HERE)]
    total = pltpu.roll(both, shifts[0], 1)[:IZ] + pltpu.roll(both, shifts[1], 1)[IZ:]
    for tile in range(IX // 128):
        out_ref[tile] = total[:, tile * 128 : (tile + 1) * 128] * scale


def focus(raw, band_bins, probe_index, tx_coord):
    even, odd = time_tables()
    vmem = pl.BlockSpec(memory_space=pltpu.VMEM)
    smem = pl.BlockSpec(memory_space=pltpu.SMEM)
    return pl.pallas_call(
        focus_kernel,
        out_shape=jax.ShapeDtypeStruct((IX // 128, IZ, 128), jnp.float32),
        in_specs=[smem, smem] + [vmem] * 7,
        out_specs=vmem,
        scratch_shapes=[
            pltpu.VMEM((POS_HERE * NE, NT), jnp.bfloat16),
            pltpu.VMEM((POS_HERE, 8, 128, 2 * NE), jnp.bfloat16),
            pltpu.VMEM((POS_HERE * IZ, 8, 128, 2 * NE), jnp.bfloat16),
            pltpu.VMEM((CENTRES, 16), jnp.float32),
            pltpu.VMEM((IX // 128, POS_HERE * IZ, 2, 8, 128), jnp.float32),
            pltpu.VMEM((IX // 128, POS_HERE * IZ, 2, 8, 128), jnp.float32),
            pltpu.VMEM((IX // 128, POS_HERE * IZ, 128), jnp.float32),
        ],
        compiler_params=pltpu.CompilerParams(vmem_limit_bytes=48 * 1024 * 1024),
        name="focus",
    )(
        probe_index,
        tx_coord,
        band_bins.reshape(1, NF),
        raw.reshape(POS_HERE * NE, NT),
        jnp.asarray(even),
        jnp.asarray(odd),
        jnp.asarray(element_table()),
        jnp.asarray(column_table()),
        jnp.asarray(depth_table()),
    )


MESH = pl.DeviceIdType.MESH


def combine_kernel(freqs, partial_ref, out_ref, inbox, middle, inbox2, send, recv, send2, recv2):
    section, freq, core = lax.axis_index("section"), lax.axis_index("freq"), lax.axis_index("pos")
    y = section * 2 + freq // 32
    x = freq // 8 % 4
    z = freq % 8
    plane = y * 4 + x
    pencil = z * 2 + core

    def plane_device(index):
        yy, xx = index // 4, index % 4
        return (yy // 2, yy % 2 * 32 + xx * 8 + z, core)

    def pencil_device(index):
        return (section, freq // 8 * 8 + index // 2, index % 2)

    barrier = pltpu.get_barrier_semaphore()
    for step in range(1, 16):
        pl.semaphore_signal(barrier, inc=1, device_id=plane_device((plane + step) % 16), device_id_type=MESH)
        pl.semaphore_signal(barrier, inc=1, device_id=pencil_device((pencil + step) % 16), device_id_type=MESH)
    pl.semaphore_wait(barrier, 30)

    copies = []
    for step in range(1, 16):
        to = (plane + step) % 16
        copy = pltpu.make_async_remote_copy(
            src_ref=partial_ref.at[to // 4],
            dst_ref=inbox.at[step - 1],
            send_sem=send.at[step - 1],
            recv_sem=recv.at[step - 1],
            device_id=plane_device(to),
            device_id_type=MESH,
        )
        copy.start()
        copies.append(copy)
    total = partial_ref[y]
    for step in range(1, 16):
        copies[step - 1].wait_recv()
        total = total + inbox[step - 1]
    middle[...] = total
    copies2 = []
    for step in range(1, 16):
        copy = pltpu.make_async_remote_copy(
            src_ref=middle,
            dst_ref=inbox2.at[step - 1],
            send_sem=send2.at[step - 1],
            recv_sem=recv2.at[step - 1],
            device_id=pencil_device((pencil + step) % 16),
            device_id_type=MESH,
        )
        copy.start()
        copies2.append(copy)
    for step in range(1, 16):
        copies2[step - 1].wait_recv()
        total = total + inbox2[step - 1]
    out_ref[...] = pltpu.roll(total, (128 - (x * 32 + z * 4)) % 128, 1)
    for copy in copies + copies2:
        copy.wait_send()


def combine(partial):
    vmem = pl.BlockSpec(memory_space=pltpu.VMEM)
    tile = (IZ, 128)
    return pl.pallas_call(
        functools.partial(combine_kernel, 64),
        out_shape=jax.ShapeDtypeStruct(tile, jnp.float32),
        in_specs=[vmem],
        out_specs=vmem,
        scratch_shapes=[
            pltpu.VMEM((15, *tile), jnp.float32),
            pltpu.VMEM(tile, jnp.float32),
            pltpu.VMEM((15, *tile), jnp.float32),
            pltpu.SemaphoreType.DMA((15,)),
            pltpu.SemaphoreType.DMA((15,)),
            pltpu.SemaphoreType.DMA((15,)),
            pltpu.SemaphoreType.DMA((15,)),
        ],
        compiler_params=pltpu.CompilerParams(collective_id=0, has_side_effects=True),
        name="combine",
    )(partial)


def per_device(raw_capture, band_bins, probe_index):
    transmitter = lax.axis_index(("section", "freq")).astype(jnp.float32)
    tx_coord = (transmitter - (NE - 1) / 2.0).reshape(1)
    partial = focus(raw_capture, band_bins, probe_index, tx_coord)
    return combine(partial)[:, :4]


def solution(mesh):
    in_specs = (P("pos", ("section", "freq"), None, None), P(), P("pos"))
    out_specs = P(None, ("section", "freq"))
    return jax.shard_map(
        per_device, mesh=mesh, in_specs=in_specs, out_specs=out_specs, check_vma=False
    )
```

time: 666 us -> 44 us (0.07)
  blocking collectives: 352 us -> 0 us
  other arithmetic: 212 us -> 0 us
  matrix products: 37.3 us -> 0 us
  Pallas kernels: 0 us -> 35.4 us
  waiting for transfers between devices: 26.3 us -> 0 us
  starting transfers between devices: 16.3 us -> 0 us
    unnamed x1 -> x0, blocking collectives: 292 us -> none
    another operation x11 -> x0, other arithmetic: 141 us -> none
    reduce_sum x8 -> x0, other arithmetic: 70.4 us -> none  [focus_bin(): jnp.sum(jnp.cos(send_phase) * field_sum[:, :pixels] - jnp.sin(send_phase)...]
    psum x1 -> x0, blocking collectives: 60.1 us -> none  [per_device(): panel_sum = lax.psum(partial_image, 'pos')]
    dot_general x24 -> x0, matrix products: 37.3 us -> none  [the longest x16 26.8 us: focus_bin(): jnp.dot(spectrum, recv_table, preferred_element_type=jnp.float32)]
    pallas_call x0 -> x2, Pallas kernels: none -> 35.4 us  [the longest x1 21.3 us: combine(): pl.pallas_call(functools.partial(combine_kernel, 64), out_shape=jax.Shape...]
    all_to_all x1 -> x0, waiting for transfers between devices: 26.3 us -> none  [per_device(): lax.all_to_all(wavefield, ('section', 'freq'), split_axis=0, concat_axis=...]
    all_to_all x1 -> x0, starting transfers between devices: 16.3 us -> none  [per_device(): lax.all_to_all(wavefield, ('section', 'freq'), split_axis=0, concat_axis=...]
  transfers between devices with their start and end apart: 1 -> 0, of which waited for: 1 -> 0; matrix products, arithmetic and copies ran while one was open for 0% -> 0% of each run, Pallas kernels for 0% -> 0%
where the time goes in v1:
time: 44 us; the launch traced here: 43.7 us
  Pallas kernels  35.4 us (80%)
  local copies, waits for them, and re-layouts  8.31 us (19%)
    pallas_call x1, Pallas kernels, combine(): pl.pallas_call(functools.partial(combine_kernel, 64), out_shape=jax.Shape...  21.3 us
    pallas_call x1, Pallas kernels, focus(): pl.pallas_call(focus_kernel, out_shape=jax.ShapeDtypeStruct((IX // 128, I...  14.1 us
    unnamed x15, local copies, waits for them, and re-layouts  8.31 us

profile of v1, /device:TPU:1, one launch (start us, length us, event | category | flops | bytes accessed | tf_op | source)
XLA Modules:
  0.0 43.7 jit_solution(1645951046182392824)
XLA Ops:
  0.0 0.0 copy-start
  0.0 1.6 %copy-done = bf16[2,1,128,4096]{3,2,1,0:T(8,128)(2,1)S(1)} copy-done((bf16[2,1,128,4096]{3,2,1,0:T(8,128)(2,1)S(1)}, bf16[2,1,128,4096]{3,2,1,0:T(8,128)(2,1)}, u32[]{:S(2)}) %copy-start) | copy-done | bytes 2097176
  1.6 0.0 copy-start.1
  1.6 1.6 %copy-done.1 = bf16[2,512,1024]{2,1,0:T(8,128)(2,1)S(1)} copy-done((bf16[2,512,1024]{2,1,0:T(8,128)(2,1)S(1)}, bf16[2,512,1024]{2,1,0:T(8,128)(2,1)}, u32[]{:S(2)}) %copy-start.1) | copy-done | bytes 2097176
  3.2 0.0 copy-start.2
  3.2 1.0 %copy-done.2 = bf16[4,256,256]{2,1,0:T(8,128)(2,1)S(1)} copy-done((bf16[4,256,256]{2,1,0:T(8,128)(2,1)S(1)}, bf16[4,256,256]{2,1,0:T(8,128)(2,1)}, u32[]{:S(2)}) %copy-start.2) | copy-done | bytes 524312
  4.2 0.0 copy-start.3
  4.2 0.9 %copy-done.3 = bf16[256,256]{1,0:T(8,128)(2,1)S(1)} copy-done((bf16[256,256]{1,0:T(8,128)(2,1)S(1)}, bf16[256,256]{1,0:T(8,128)(2,1)}, u32[]{:S(2)}) %copy-start.3) | copy-done | bytes 131096
  5.1 0.0 copy-start.5
  5.1 0.7 %copy-done.5 = s32[1024]{0:T(1024)S(1)} copy-done((s32[1024]{0:T(1024)S(1)}, s32[1024]{0:T(1024)}, u32[]{:S(2)}) %copy-start.5) | copy-done | bytes 4120
  5.8 0.0 copy-start.6
  5.8 0.7 %copy-done.6 = s32[2]{0:T(128)S(1)} copy-done((s32[2]{0:T(128)S(1)}, s32[2]{0:T(128)}, u32[]{:S(2)}) %copy-start.6) | copy-done | bytes 32
  6.5 14.1 %focus.1.partial_ref = f32[4,4,128]{2,1,0:T(4,128)S(1)} custom-call(s32[2]{0:T(128)S(1)} %copy-done.6, f32[1]{0:T(128)} %bitcast.tx_ref, s32[1,1024]{1,0:T(1,128)S(1)} %bitcast.5, bf16[256,4096]{1,0:T(8,128)(2,1)S(1)} %bitcast.4, bf16[2,512,1024]{2,1,0:T(8,128)(2,1)S(1)} %copy-done.1, bf16[512,2048]{1,0:T(8,128)(2,1)} %constant.26.clone.odd_ref, ...), custom_call_target="tpu_custom_call" | custom-call | tf_op jit(solution)/shard_map/focus/pallas_call | solution.py:251
  20.6 0.0 copy-start.4
  20.6 0.6 %copy-done.4 = f32[4,4,128]{2,1,0:T(4,128)} copy-done((f32[4,4,128]{2,1,0:T(4,128)}, f32[4,4,128]{2,1,0:T(4,128)S(1)}, u32[]{:S(2)}) %copy-start.4) | copy-done | bytes 8216
  21.2 21.3 %combine.1 = f32[4,128]{1,0:T(4,128)} custom-call(f32[4,4,128]{2,1,0:T(4,128)} %copy-done.4), custom_call_target="tpu_custom_call" | custom-call | tf_op jit(solution)/shard_map/combine/pallas_call | solution.py:345
  42.5 1.2 %copy.10 = f32[4,4]{1,0:T(4,128)} copy(f32[4,4]{1,0:T(4,128)} %bitcast.6) | data formatting | bytes 128
Async XLA Ops:
  0.0 1.6 %copy-start = (bf16[2,1,128,4096]{3,2,1,0:T(8,128)(2,1)S(1)}, bf16[2,1,128,4096]{3,2,1,0:T(8,128)(2,1)}, u32[]{:S(2)}) copy-start(bf16[2,1,128,4096]{3,2,1,0:T(8,128)(2,1)} %param.8) | copy-start | bytes 6291460
  1.6 1.6 %copy-start.1 = (bf16[2,512,1024]{2,1,0:T(8,128)(2,1)S(1)}, bf16[2,512,1024]{2,1,0:T(8,128)(2,1)}, u32[]{:S(2)}) copy-start(bf16[2,512,1024]{2,1,0:T(8,128)(2,1)} %constant.25.clone.even_ref) | copy-start | bytes 6291460
  3.2 1.0 %copy-start.2 = (bf16[4,256,256]{2,1,0:T(8,128)(2,1)S(1)}, bf16[4,256,256]{2,1,0:T(8,128)(2,1)}, u32[]{:S(2)}) copy-start(bf16[4,256,256]{2,1,0:T(8,128)(2,1)} %constant.28.clone.column_ref) | copy-start | bytes 1572868
  4.2 0.9 %copy-start.3 = (bf16[256,256]{1,0:T(8,128)(2,1)S(1)}, bf16[256,256]{1,0:T(8,128)(2,1)}, u32[]{:S(2)}) copy-start(bf16[256,256]{1,0:T(8,128)(2,1)} %constant.27.clone.element_ref) | copy-start | bytes 393220
  5.1 0.7 %copy-start.5 = (s32[1024]{0:T(1024)S(1)}, s32[1024]{0:T(1024)}, u32[]{:S(2)}) copy-start(s32[1024]{0:T(1024)} %param.9) | copy-start | bytes 12292
  5.8 0.7 %copy-start.6 = (s32[2]{0:T(128)S(1)}, s32[2]{0:T(128)}, u32[]{:S(2)}) copy-start(s32[2]{0:T(128)} %probe_ref.1) | copy-start | bytes 28
  20.6 0.6 %copy-start.4 = (f32[4,4,128]{2,1,0:T(4,128)}, f32[4,4,128]{2,1,0:T(4,128)S(1)}, u32[]{:S(2)}) copy-start(f32[4,4,128]{2,1,0:T(4,128)S(1)} %focus.1.partial_ref) | copy-start | bytes 24580

commit v2 on v1

v2 whole, which is shorter than its diff:
```python
import math

import jax
import jax.numpy as jnp
import ml_dtypes
import numpy as np
from jax import lax
from jax.experimental import pallas as pl
from jax.experimental.pallas import tpu as pltpu
from jax.sharding import PartitionSpec as P

NE = 128
NT = 4096
NF = 1024
IX = 512
IZ = 4
POS_HERE = 2
QUARTER = NT // 4
LOWEST = 64
CENTRES = 48
SPACING = 20
FIRST = LOWEST + 9
GROUPS = 10
TILES = IX // 128
MESH = pl.DeviceIdType.MESH

wave_speed = 0.5
pixel_pitch = 0.25
depth_start = 20.0
probe_anchor = 32

EVEN = ((-9, -5, -1, 3, 7), (-7, -3, 1, 5, 9))
ODD = ((-8, -4, 0, 4, 8), (-6, -2, 2, 6, 10))


def group_of(offset):
    if offset in (0, 10):
        return GROUPS - 1, CENTRES * (offset // 10)
    return abs(offset) - 1, 0 if offset > 0 else CENTRES


def offsets_of(group):
    return (group + 1, -group - 1) if group < GROUPS - 1 else (0, 10)


def time_tables():
    samples = np.arange(QUARTER)
    centres = FIRST + SPACING * np.arange(CENTRES)

    def parts(offsets):
        bins = np.concatenate([centres + offset for offset in offsets])
        angle = 2.0 * np.pi * (bins[:, None] * samples[None, :] % NT) / NT
        return np.cos(angle), -np.sin(angle)

    even = np.stack([np.concatenate(parts(offsets), axis=0) for offsets in EVEN])
    re1, im1 = parts(ODD[0])
    re3, im3 = parts(ODD[1])
    odd = np.concatenate(
        [np.concatenate([re1, im1], axis=1), np.concatenate([im3, re3], axis=1)], axis=0
    )
    return even.astype(ml_dtypes.bfloat16), odd.astype(ml_dtypes.bfloat16)


def element_table():
    pos = np.arange(NE) - (NE - 1) / 2.0
    angle = pos[:, None] * (np.arange(NE) - NE // 2)[None, :] * (2.0 * np.pi / NE)
    c, s = np.cos(angle), np.sin(angle)
    table = np.concatenate([np.concatenate([c, -s], axis=1), np.concatenate([s, c], axis=1)], axis=0)
    return table.astype(ml_dtypes.bfloat16)


def column_table():
    order = np.arange(NE) - NE // 2
    angle = 2.0 * np.pi * (order[:, None] * np.arange(IX)[None, :] % IX) / IX
    cosine, sine = np.cos(angle), np.sin(angle)
    tiles = []
    for start in range(0, IX, 128):
        c, s = cosine[:, start : start + 128], sine[:, start : start + 128]
        tiles.append(
            np.concatenate([np.concatenate([c, s], axis=1), np.concatenate([-s, c], axis=1)], axis=0)
        )
    return np.stack(tiles).astype(ml_dtypes.bfloat16)


def depth_table():
    centres = FIRST + SPACING * np.arange(CENTRES)
    wavenumber = (np.arange(NE) - NE // 2) * (2.0 * np.pi / NE)

    def parts(offset):
        k = (centres + offset)[:, None] * (2.0 * np.pi / NT) / wave_speed
        vertical = np.sqrt(np.maximum(k * k - wavenumber[None, :] ** 2, 0.0))
        weight = vertical / k
        first = weight * np.exp(1j * vertical * depth_start)
        step = np.exp(1j * vertical * pixel_pitch)
        return np.stack([first.real, first.imag, step.real, step.imag])

    groups = [
        np.concatenate([parts(offset) for offset in offsets_of(group)], axis=1) for group in range(GROUPS)
    ]
    return np.stack(groups, axis=1).astype(np.float32)


def turn_pair(turns):
    x = turns - jnp.floor(turns + 0.5)
    square = x * x
    sine = jnp.full_like(x, math.pi**13 / math.factorial(13))
    for power in (11, 9, 7, 5, 3, 1):
        sign = 1.0 if power % 4 == 1 else -1.0
        sine = sine * square + sign * math.pi**power / math.factorial(power)
    sine = sine * x
    cosine = jnp.full_like(x, math.pi**12 / math.factorial(12))
    for power in (10, 8, 6, 4, 2, 0):
        sign = 1.0 if power % 4 == 0 else -1.0
        cosine = cosine * square + sign * math.pi**power / math.factorial(power)
    return 1.0 - 2.0 * sine * sine, 2.0 * sine * cosine


def transposed_dot(a, b):
    return lax.dot_general(a, b, (((1,), (1,)), ((), ())), preferred_element_type=jnp.float32)


def hops(count, delta):
    return min(delta, count - delta)


PLANE = sorted(
    [(dy, dx) for dy in range(4) for dx in range(4) if dy or dx],
    key=lambda d: -(hops(4, d[0]) + hops(4, d[1])),
)
PENCIL = sorted(
    [(dz, dc) for dz in range(8) for dc in range(2) if dz or dc],
    key=lambda d: -(2 * hops(8, d[0]) + d[1]),
)


def focus_kernel(
    probe_ref, bins_ref, raw_hbm, even_hbm, odd_hbm, element_hbm, column_hbm, depth_hbm,
    out_ref,
    raw_ref, even_ref, odd_ref, element_ref, column_ref, depth_ref, loaded,
    negative, spectra, rows, counts, near, far, image,
    partial, inbox, middle, inbox2, send, recv, send2, recv2,
):
    section, freq, core = lax.axis_index("section"), lax.axis_index("freq"), lax.axis_index("pos")
    y, x_chip, z_chip = section * 2 + (freq >> 5), (freq >> 3) & 3, freq & 7

    def plane_device(dy, dx):
        yy, xx = (y + dy) & 3, (x_chip + dx) & 3
        return (yy >> 1, (yy & 1) * 32 + xx * 8 + z_chip, core)

    def pencil_device(dz, dc):
        return (section, (freq & 56) + ((z_chip + dz) & 7), (core + dc) & 1)

    def load(index, source, target):
        return pltpu.make_async_copy(source, target, loaded.at[index])

    loads = [
        load(0, raw_hbm, raw_ref),
        load(1, even_hbm.at[0], even_ref.at[0]),
        load(2, even_hbm.at[1], even_ref.at[1]),
        load(3, odd_hbm, odd_ref),
        load(4, element_hbm, element_ref),
        load(5, depth_hbm, depth_ref),
        load(6, column_hbm, column_ref),
    ]
    for copy in loads[:2]:
        copy.start()

    barrier = pltpu.get_barrier_semaphore()
    for step in PLANE:
        pl.semaphore_signal(barrier, inc=1, device_id=plane_device(*step), device_id_type=MESH)
    for step in PENCIL:
        pl.semaphore_signal(barrier, inc=1, device_id=pencil_device(*step), device_id_type=MESH)

    bins = bins_ref[...] - LOWEST
    centre = (bins * 3277) >> 16
    offset = bins - SPACING * centre
    is_centre = jnp.where(lax.broadcasted_iota(jnp.int32, (CENTRES, NF), 0) == centre, 1.0, 0.0)
    is_offset = jnp.where(lax.broadcasted_iota(jnp.int32, (32, NF), 0) == offset, 1.0, 0.0)
    counts[...] = transposed_dot(is_centre.astype(jnp.bfloat16), is_offset.astype(jnp.bfloat16))

    tx_coord = (section * 64 + freq).astype(jnp.float32) - (NE - 1) / 2.0
    sub = lax.broadcasted_iota(jnp.int32, (16, 128), 0).astype(jnp.float32)
    near_powers = jnp.where(sub < 10.0, sub + 1.0, SPACING * 8.0)
    far_powers = FIRST + SPACING * sub[:8]
    lane = lax.broadcasted_iota(jnp.int32, (8, 128), 1)
    for p in range(POS_HERE):
        shift = 4 * (probe_ref[p] + probe_anchor)
        centre_here = (probe_ref[p] + probe_anchor).astype(jnp.float32)
        for tile in range(TILES):
            column = ((lane + (128 * tile + shift)) & (IX - 1)).astype(jnp.float32)
            x = (pixel_pitch * column - centre_here) - tx_coord
            for k in range(IZ):
                z = depth_start + pixel_pitch * k
                turns = jnp.sqrt(x * x + z * z) * (1.0 / (NT * wave_speed))
                c, s = turn_pair(jnp.concatenate([turns, turns], axis=0) * near_powers)
                near[tile, p * IZ + k, 0], near[tile, p * IZ + k, 1] = c, s
                c, s = turn_pair(turns * far_powers)
                far[tile, p * IZ + k, 0], far[tile, p * IZ + k, 1] = c, s

    def quarters(signs):
        return jnp.concatenate(
            [
                (raw_ref if sign > 0 else negative)[:, q * QUARTER : (q + 1) * QUARTER]
                for q, sign in enumerate(signs)
            ],
            axis=1,
        )

    def keep(values, offsets, part):
        for index, offset in enumerate(offsets):
            group, row = group_of(offset)
            for p in range(POS_HERE):
                spectra[p, group, row : row + CENTRES, part * NE : (part + 1) * NE] = values[
                    index * CENTRES : (index + 1) * CENTRES, p * NE : (p + 1) * NE
                ]

    def filtered(group, p):
        scales = [counts[:, 9 + o : 10 + o] for o in offsets_of(group)]
        field = jnp.dot(spectra[p, group], element_ref[...], preferred_element_type=jnp.float32)
        field = field.astype(jnp.bfloat16)
        for block in range(0, CENTRES, 16):
            parts = []
            for half in range(2):
                at = slice(half * CENTRES + block, half * CENTRES + block + 16)
                scale = scales[half][block : block + 16]
                re = field[at, :NE].astype(jnp.float32) * scale
                im = field[at, NE:].astype(jnp.float32) * scale
                cosine, sine = depth_ref[0, group, at, :], depth_ref[1, group, at, :]
                parts.append([re * cosine - im * sine, re * sine + im * cosine])
            for k in range(IZ):
                if k > 0:
                    for half in range(2):
                        at = slice(half * CENTRES + block, half * CENTRES + block + 16)
                        cosine, sine = depth_ref[2, group, at, :], depth_ref[3, group, at, :]
                        re, im = parts[half]
                        parts[half] = [re * cosine - im * sine, re * sine + im * cosine]
                (re, im), (re_low, im_low) = parts
                if group < GROUPS - 1:
                    values = (re + re_low, im + im_low, re - re_low, im - im_low)
                else:
                    values = (re, im, re_low, im_low)
                re, im, re_low, im_low = [value.astype(jnp.bfloat16) for value in values]
                top = slice(block, block + 16)
                low = slice(CENTRES + block, CENTRES + block + 16)
                rows[p * IZ + k, group, top, :NE] = re
                rows[p * IZ + k, group, top, NE:] = im
                rows[p * IZ + k, group, low, :NE] = re_low
                rows[p * IZ + k, group, low, NE:] = im_low

    half_rows = 5 * CENTRES
    loads[0].wait()
    loads[1].wait()
    for copy in loads[2:]:
        copy.start()
    negative[...] = -raw_ref[...]
    for index, signs in enumerate(((1, 1, 1, 1), (1, -1, 1, -1))):
        if index > 0:
            loads[2].wait()
        table = even_ref[index]
        out = transposed_dot(jnp.concatenate([table] * 4, axis=1), quarters(signs)).astype(jnp.bfloat16)
        keep(out[:half_rows], EVEN[index], 0)
        keep(out[half_rows:], EVEN[index], 1)
    for copy in loads[3:]:
        copy.wait()
    left, right = odd_ref[:, :QUARTER], odd_ref[:, QUARTER:]
    out = transposed_dot(
        jnp.concatenate([left, right, left, right], axis=1), quarters((1, 1, -1, -1))
    ).astype(jnp.bfloat16)
    keep(out[:half_rows], ODD[0], 0)
    keep(out[half_rows:], ODD[1], 1)
    out = transposed_dot(
        jnp.concatenate([right, left, right, left], axis=1), quarters((1, -1, -1, 1))
    ).astype(jnp.bfloat16)
    keep(out[:half_rows], ODD[0], 1)
    keep(out[half_rows:], ODD[1], 0)
    for p in range(POS_HERE):
        for group in range(GROUPS):
            filtered(group, p)

    @pl.loop(0, TILES)
    def _(tile):
        weights = column_ref[tile]
        for pk in range(POS_HERE * IZ):
            total_re = jnp.zeros((CENTRES, 128), jnp.float32)
            total_im = jnp.zeros((CENTRES, 128), jnp.float32)
            for group in range(GROUPS):
                both = jnp.dot(rows[pk, group], weights, preferred_element_type=jnp.float32)
                c, s = near[tile, pk, 0, group : group + 1, :], near[tile, pk, 1, group : group + 1, :]
                low_re, low_im = both[CENTRES:, :128], both[CENTRES:, 128:]
                if group < GROUPS - 1:
                    total_re += c * both[:CENTRES, :128] - s * low_im
                    total_im += c * both[:CENTRES, 128:] + s * low_re
                else:
                    total_re += both[:CENTRES, :128] + (c * low_re - s * low_im)
                    total_im += both[:CENTRES, 128:] + (c * low_im + s * low_re)
            jump_cos = jnp.broadcast_to(near[tile, pk, 0, 10:11, :], (8, 128))
            jump_sin = jnp.broadcast_to(near[tile, pk, 1, 10:11, :], (8, 128))
            re, im = total_re[CENTRES - 8 :], total_im[CENTRES - 8 :]
            for g in range(CENTRES // 8 - 2, -1, -1):
                re, im = (
                    re * jump_cos - im * jump_sin + total_re[8 * g : 8 * g + 8],
                    re * jump_sin + im * jump_cos + total_im[8 * g : 8 * g + 8],
                )
            value = re * far[tile, pk, 0] - im * far[tile, pk, 1]
            image[tile, pk : pk + 1, :] = jnp.sum(value, axis=0, keepdims=True)

    both = jnp.concatenate([image[tile] for tile in range(TILES)], axis=1)
    is_first = lax.broadcasted_iota(jnp.int32, (POS_HERE * IZ, IX), 0) < IZ
    turn = jnp.where(is_first, probe_ref[0] + probe_anchor, probe_ref[1] + probe_anchor)
    for bit in range(7):
        both = jnp.where(((turn >> bit) & 1) == 1, pltpu.roll(both, 4 << bit, 1), both)
    scale = 1.0 / math.sqrt(float(NT * NE**3 * NF * 4))
    for tile in range(TILES):
        columns = slice(tile * 128, (tile + 1) * 128)
        partial[tile] = (both[:IZ, columns] + both[IZ:, columns]) * scale

    pl.semaphore_wait(barrier, len(PLANE) + len(PENCIL))
    copies = []
    for index, step in enumerate(PLANE):
        copy = pltpu.make_async_remote_copy(
            src_ref=partial.at[(y + step[0]) & 3],
            dst_ref=inbox.at[index],
            send_sem=send.at[index],
            recv_sem=recv.at[index],
            device_id=plane_device(*step),
            device_id_type=MESH,
        )
        copy.start()
        copies.append(copy)
    total = partial[y]
    for index in reversed(range(len(PLANE))):
        copies[index].wait_recv()
        total = total + inbox[index]
    middle[...] = total
    copies2 = []
    for index, step in enumerate(PENCIL):
        copy = pltpu.make_async_remote_copy(
            src_ref=middle,
            dst_ref=inbox2.at[index],
            send_sem=send2.at[index],
            recv_sem=recv2.at[index],
            device_id=pencil_device(*step),
            device_id_type=MESH,
        )
        copy.start()
        copies2.append(copy)
    for index in reversed(range(len(PENCIL))):
        copies2[index].wait_recv()
        total = total + inbox2[index]
    out_ref[...] = pltpu.roll(total, (128 - (x_chip * 32 + z_chip * 4)) & 127, 1)
    for copy in copies + copies2:
        copy.wait_send()


def focus(raw, band_bins, probe_index):
    even, odd = time_tables()
    tables = [even, odd, element_table(), column_table(), depth_table()]
    vmem = pl.BlockSpec(memory_space=pltpu.VMEM)
    smem = pl.BlockSpec(memory_space=pltpu.SMEM)
    hbm = pl.BlockSpec(memory_space=pltpu.HBM)
    held = [pltpu.VMEM((POS_HERE * NE, NT), jnp.bfloat16)]
    held += [pltpu.VMEM(table.shape, table.dtype) for table in tables]
    tile = (IZ, 128)
    return pl.pallas_call(
        focus_kernel,
        out_shape=jax.ShapeDtypeStruct(tile, jnp.float32),
        in_specs=[smem, vmem] + [hbm] * 6,
        out_specs=vmem,
        scratch_shapes=[
            *held,
            pltpu.SemaphoreType.DMA((7,)),
            pltpu.VMEM((POS_HERE * NE, NT), jnp.bfloat16),
            pltpu.VMEM((POS_HERE, GROUPS, 2 * CENTRES, 2 * NE), jnp.bfloat16),
            pltpu.VMEM((POS_HERE * IZ, GROUPS, 2 * CENTRES, 2 * NE), jnp.bfloat16),
            pltpu.VMEM((CENTRES, 32), jnp.float32),
            pltpu.VMEM((TILES, POS_HERE * IZ, 2, 16, 128), jnp.float32),
            pltpu.VMEM((TILES, POS_HERE * IZ, 2, 8, 128), jnp.float32),
            pltpu.VMEM((TILES, POS_HERE * IZ, 128), jnp.float32),
            pltpu.VMEM((TILES, *tile), jnp.float32),
            pltpu.VMEM((15, *tile), jnp.float32),
            pltpu.VMEM(tile, jnp.float32),
            pltpu.VMEM((15, *tile), jnp.float32),
            pltpu.SemaphoreType.DMA((15,)),
            pltpu.SemaphoreType.DMA((15,)),
            pltpu.SemaphoreType.DMA((15,)),
            pltpu.SemaphoreType.DMA((15,)),
        ],
        compiler_params=pltpu.CompilerParams(
            collective_id=0, has_side_effects=True, vmem_limit_bytes=63 * 1024 * 1024
        ),
        name="focus",
    )(
        probe_index,
        band_bins.reshape(1, NF),
        raw.reshape(POS_HERE * NE, NT),
        *[jnp.asarray(table) for table in tables],
    )


def per_device(raw_capture, band_bins, probe_index):
    return focus(raw_capture, band_bins, probe_index)[:, :4]


def solution(mesh):
    in_specs = (P("pos", ("section", "freq"), None, None), P(), P("pos"))
    out_specs = P(None, ("section", "freq"))
    return jax.shard_map(
        per_device, mesh=mesh, in_specs=in_specs, out_specs=out_specs, check_vma=False
    )
```

time: 44 us -> 38 us (0.86)
  local copies, waits for them, and re-layouts: 8.31 us -> 1.26 us
  Pallas kernels: 35.4 us -> 36.5 us
    unnamed x15 -> x1, local copies, waits for them, and re-layouts: 8.31 us -> 1.26 us
    pallas_call x2 -> x1, Pallas kernels: 35.4 us -> 36.5 us  [focus(): pl.pallas_call(focus_kernel, out_shape=jax.ShapeDtypeStruct(tile, jnp.flo...]
where the time goes in v2:
time: 38 us; the launch traced here: 37.8 us
  Pallas kernels  36.5 us (96%)
  local copies, waits for them, and re-layouts  1.26 us (3%)
    pallas_call x1, Pallas kernels, focus(): pl.pallas_call(focus_kernel, out_shape=jax.ShapeDtypeStruct(tile, jnp.flo...  36.5 us
    unnamed x1, local copies, waits for them, and re-layouts  1.26 us

profile of v2, /device:TPU:1, one launch (start us, length us, event | category | flops | bytes accessed | tf_op | source)
XLA Modules:
  0.0 37.8 jit_solution(6666056973835662197)
XLA Ops:
  0.0 36.5 %focus.1 = f32[4,128]{1,0:T(4,128)} custom-call(s32[2]{0:T(128)} %probe_ref.1, s32[1,1024]{1,0:T(1,128)} %bitcast.5, bf16[256,4096]{1,0:T(8,128)(2,1)} %bitcast.3, bf16[2,480,1024]{2,1,0:T(8,128)(2,1)} %constant.10.clone.even_hbm, bf16[480,2048]{1,0:T(8,128)(2,1)} %constant.11.clone.odd_hbm, bf16[256,256]{1,0:T(8,128)(2,1)} %constant.12.clone.element_hbm, ...), custom_call_target="tpu_custom_call" | custom-call | tf_op jit(solution)/shard_map/focus/pallas_call | solution.py:364
  36.5 1.3 %copy.10 = f32[4,4]{1,0:T(4,128)} copy(f32[4,4]{1,0:T(4,128)} %bitcast.4) | data formatting | bytes 128

commit v3 on v2

--- a/solution.py
+++ b/solution.py
@@ -20,7 +20,9 @@
 CENTRES = 48
 SPACING = 20
 FIRST = LOWEST + 9
-GROUPS = 10
+PAIRS = ((1, -1), (3, -3), (5, -5), (7, -7), (9, -9), (2, -2), (4, -4), (6, -6), (8, -8), (0, 10))
+GROUPS = len(PAIRS)
+HALF = GROUPS // 2
 TILES = IX // 128
 MESH = pl.DeviceIdType.MESH
 
@@ -34,13 +36,8 @@
 
 
 def group_of(offset):
-    if offset in (0, 10):
-        return GROUPS - 1, CENTRES * (offset // 10)
-    return abs(offset) - 1, 0 if offset > 0 else CENTRES
-
-
-def offsets_of(group):
-    return (group + 1, -group - 1) if group < GROUPS - 1 else (0, 10)
+    group = [offset in pair for pair in PAIRS].index(True)
+    return group, CENTRES * PAIRS[group].index(offset)
 
 
 def time_tables():
@@ -95,7 +92,7 @@
         return np.stack([first.real, first.imag, step.real, step.imag])
 
     groups = [
-        np.concatenate([parts(offset) for offset in offsets_of(group)], axis=1) for group in range(GROUPS)
+        np.concatenate([parts(offset) for offset in pair], axis=1) for pair in PAIRS
     ]
     return np.stack(groups, axis=1).astype(np.float32)
 
@@ -150,19 +147,21 @@
     def pencil_device(dz, dc):
         return (section, (freq & 56) + ((z_chip + dz) & 7), (core + dc) & 1)
 
-    def load(index, source, target):
-        return pltpu.make_async_copy(source, target, loaded.at[index])
-
-    loads = [
-        load(0, raw_hbm, raw_ref),
-        load(1, even_hbm.at[0], even_ref.at[0]),
-        load(2, even_hbm.at[1], even_ref.at[1]),
-        load(3, odd_hbm, odd_ref),
-        load(4, element_hbm, element_ref),
-        load(5, depth_hbm, depth_ref),
-        load(6, column_hbm, column_ref),
-    ]
-    for copy in loads[:2]:
+    def pieces(first, source, target, count):
+        step = source.shape[0] // count
+        return [
+            pltpu.make_async_copy(
+                source.at[pl.ds(i * step, step)], target.at[pl.ds(i * step, step)], loaded.at[first + i]
+            )
+            for i in range(count)
+        ]
+
+    raw_loads = pieces(0, raw_hbm, raw_ref, 4)
+    even_loads = [pieces(4 + 2 * i, even_hbm.at[i], even_ref.at[i], 2) for i in range(2)]
+    odd_loads = pieces(8, odd_hbm, odd_ref, 2)
+    filter_loads = pieces(10, element_hbm, element_ref, 1) + pieces(11, depth_hbm, depth_ref, 4)
+    column_loads = pieces(15, column_hbm, column_ref, 1)
+    for copy in raw_loads + even_loads[0]:
         copy.start()
 
     barrier = pltpu.get_barrier_semaphore()
@@ -214,78 +213,94 @@
                     index * CENTRES : (index + 1) * CENTRES, p * NE : (p + 1) * NE
                 ]
 
-    def filtered(group, p):
-        scales = [counts[:, 9 + o : 10 + o] for o in offsets_of(group)]
-        field = jnp.dot(spectra[p, group], element_ref[...], preferred_element_type=jnp.float32)
-        field = field.astype(jnp.bfloat16)
-        for block in range(0, CENTRES, 16):
-            parts = []
-            for half in range(2):
-                at = slice(half * CENTRES + block, half * CENTRES + block + 16)
-                scale = scales[half][block : block + 16]
-                re = field[at, :NE].astype(jnp.float32) * scale
-                im = field[at, NE:].astype(jnp.float32) * scale
-                cosine, sine = depth_ref[0, group, at, :], depth_ref[1, group, at, :]
-                parts.append([re * cosine - im * sine, re * sine + im * cosine])
-            for k in range(IZ):
-                if k > 0:
-                    for half in range(2):
-                        at = slice(half * CENTRES + block, half * CENTRES + block + 16)
-                        cosine, sine = depth_ref[2, group, at, :], depth_ref[3, group, at, :]
-                        re, im = parts[half]
-                        parts[half] = [re * cosine - im * sine, re * sine + im * cosine]
-                (re, im), (re_low, im_low) = parts
-                if group < GROUPS - 1:
-                    values = (re + re_low, im + im_low, re - re_low, im - im_low)
-                else:
-                    values = (re, im, re_low, im_low)
-                re, im, re_low, im_low = [value.astype(jnp.bfloat16) for value in values]
-                top = slice(block, block + 16)
-                low = slice(CENTRES + block, CENTRES + block + 16)
-                rows[p * IZ + k, group, top, :NE] = re
-                rows[p * IZ + k, group, top, NE:] = im
-                rows[p * IZ + k, group, low, :NE] = re_low
-                rows[p * IZ + k, group, low, NE:] = im_low
+    def filtered(start, p):
+        groups = range(start, start + HALF)
+        fields = spectra[p, start : start + HALF].reshape(HALF * 2 * CENTRES, 2 * NE)
+        fields = jnp.dot(fields, element_ref[...], preferred_element_type=jnp.float32)
+        fields = fields.astype(jnp.bfloat16)
+        for group in groups:
+            scales = [counts[:, 9 + o : 10 + o] for o in PAIRS[group]]
+            for block in range(0, CENTRES, 16):
+                parts = []
+                for half in range(2):
+                    row = half * CENTRES + block
+                    at = slice(row, row + 16)
+                    field = fields[(group - start) * 2 * CENTRES + row :][:16].astype(jnp.float32)
+                    scale = scales[half][block : block + 16]
+                    re, im = field[:, :NE] * scale, field[:, NE:] * scale
+                    cosine, sine = depth_ref[0, group, at, :], depth_ref[1, group, at, :]
+                    parts.append([re * cosine - im * sine, re * sine + im * cosine])
+                for k in range(IZ):
+                    if k > 0:
+                        for half in range(2):
+                            at = slice(half * CENTRES + block, half * CENTRES + block + 16)
+                            cosine, sine = depth_ref[2, group, at, :], depth_ref[3, group, at, :]
+                            re, im = parts[half]
+                            parts[half] = [re * cosine - im * sine, re * sine + im * cosine]
+                    (re, im), (re_low, im_low) = parts
+                    if group < GROUPS - 1:
+                        values = (re + re_low, im + im_low, re - re_low, im - im_low)
+                    else:
+                        values = (re, im, re_low, im_low)
+                    re, im, re_low, im_low = [value.astype(jnp.bfloat16) for value in values]
+                    top = slice(block, block + 16)
+                    low = slice(CENTRES + block, CENTRES + block + 16)
+                    rows[p * IZ + k, group, top, :NE] = re
+                    rows[p * IZ + k, group, top, NE:] = im
+                    rows[p * IZ + k, group, low, :NE] = re_low
+                    rows[p * IZ + k, group, low, NE:] = im_low
 
     half_rows = 5 * CENTRES
-    loads[0].wait()
-    loads[1].wait()
-    for copy in loads[2:]:
-        copy.start()
-    negative[...] = -raw_ref[...]
-    for index, signs in enumerate(((1, 1, 1, 1), (1, -1, 1, -1))):
-        if index > 0:
-            loads[2].wait()
+    left, right = slice(0, QUARTER), slice(QUARTER, 2 * QUARTER)
+
+    def even_bins(index):
         table = even_ref[index]
+        signs = (1, 1 - 2 * index, 1, 1 - 2 * index)
         out = transposed_dot(jnp.concatenate([table] * 4, axis=1), quarters(signs)).astype(jnp.bfloat16)
         keep(out[:half_rows], EVEN[index], 0)
         keep(out[half_rows:], EVEN[index], 1)
-    for copy in loads[3:]:
+
+    def odd_bins(index):
+        one, two = odd_ref[:, (left, right)[index]], odd_ref[:, (right, left)[index]]
+        signs = ((1, 1, -1, -1), (1, -1, -1, 1))[index]
+        out = transposed_dot(
+            jnp.concatenate([one, two, one, two], axis=1), quarters(signs)
+        ).astype(jnp.bfloat16)
+        keep(out[:half_rows], ODD[0], index)
+        keep(out[half_rows:], ODD[1], 1 - index)
+
+    for copy in even_loads[1]:
+        copy.start()
+    for copy in raw_loads + even_loads[0] + even_loads[1]:
         copy.wait()
-    left, right = odd_ref[:, :QUARTER], odd_ref[:, QUARTER:]
-    out = transposed_dot(
-        jnp.concatenate([left, right, left, right], axis=1), quarters((1, 1, -1, -1))
-    ).astype(jnp.bfloat16)
-    keep(out[:half_rows], ODD[0], 0)
-    keep(out[half_rows:], ODD[1], 1)
-    out = transposed_dot(
-        jnp.concatenate([right, left, right, left], axis=1), quarters((1, -1, -1, 1))
-    ).astype(jnp.bfloat16)
-    keep(out[:half_rows], ODD[0], 1)
-    keep(out[half_rows:], ODD[1], 0)
-    for p in range(POS_HERE):
-        for group in range(GROUPS):
-            filtered(group, p)
-
-    @pl.loop(0, TILES)
+    for copy in odd_loads + filter_loads + column_loads:
+        copy.start()
+    even_bins(0)
+    for q in range(1, 4):
+        negative[:, q * QUARTER : (q + 1) * QUARTER] = -raw_ref[:, q * QUARTER : (q + 1) * QUARTER]
+    even_bins(1)
+    for copy in odd_loads + filter_loads + column_loads:
+        copy.wait()
+    filtered(0, 0)
+    odd_bins(0)
+    filtered(0, 1)
+    odd_bins(1)
+    filtered(HALF, 0)
+    filtered(HALF, 1)
+
+    @pl.loop(0, TILES, unroll=TILES)
     def _(tile):
         weights = column_ref[tile]
         for pk in range(POS_HERE * IZ):
             total_re = jnp.zeros((CENTRES, 128), jnp.float32)
             total_im = jnp.zeros((CENTRES, 128), jnp.float32)
-            for group in range(GROUPS):
-                both = jnp.dot(rows[pk, group], weights, preferred_element_type=jnp.float32)
-                c, s = near[tile, pk, 0, group : group + 1, :], near[tile, pk, 1, group : group + 1, :]
+            several = rows[pk].reshape(GROUPS * 2 * CENTRES, 2 * NE)
+            several = jnp.dot(several, weights, preferred_element_type=jnp.float32)
+            for group, (offset, other) in enumerate(PAIRS):
+                first = group * 2 * CENTRES
+                both = several[first : first + 2 * CENTRES]
+                power = max(offset, other)
+                c, s = near[tile, pk, 0, power - 1 : power, :], near[tile, pk, 1, power - 1 : power, :]
                 low_re, low_im = both[CENTRES:, :128], both[CENTRES:, 128:]
                 if group < GROUPS - 1:
                     total_re += c * both[:CENTRES, :128] - s * low_im
@@ -368,7 +383,7 @@
         out_specs=vmem,
         scratch_shapes=[
             *held,
-            pltpu.SemaphoreType.DMA((7,)),
+            pltpu.SemaphoreType.DMA((16,)),
             pltpu.VMEM((POS_HERE * NE, NT), jnp.bfloat16),
             pltpu.VMEM((POS_HERE, GROUPS, 2 * CENTRES, 2 * NE), jnp.bfloat16),
             pltpu.VMEM((POS_HERE * IZ, GROUPS, 2 * CENTRES, 2 * NE), jnp.bfloat16),

time: 38 us -> 32.5 us (0.86)
  Pallas kernels: 36.5 us -> 31.1 us
    pallas_call x1, Pallas kernels: 36.5 us -> 31.1 us  [focus(): pl.pallas_call(focus_kernel, out_shape=jax.ShapeDtypeStruct(tile, jnp.flo...]
where the time goes in v3:
time: 32.5 us; the launch traced here: 32.4 us
  Pallas kernels  31.1 us (96%)
  local copies, waits for them, and re-layouts  1.26 us (4%)
    pallas_call x1, Pallas kernels, focus(): pl.pallas_call(focus_kernel, out_shape=jax.ShapeDtypeStruct(tile, jnp.flo...  31.1 us
    unnamed x1, local copies, waits for them, and re-layouts  1.26 us

profile of v3, /device:TPU:1, one launch (start us, length us, event | category | flops | bytes accessed | tf_op | source)
XLA Modules:
  0.0 32.4 jit_solution(11397252762853522090)
XLA Ops:
  0.0 31.1 %focus.1 = f32[4,128]{1,0:T(4,128)} custom-call(s32[2]{0:T(128)} %probe_ref.1, s32[1,1024]{1,0:T(1,128)} %bitcast.5, bf16[256,4096]{1,0:T(8,128)(2,1)} %bitcast.3, bf16[2,480,1024]{2,1,0:T(8,128)(2,1)} %constant.10.clone.even_hbm, bf16[480,2048]{1,0:T(8,128)(2,1)} %constant.11.clone.odd_hbm, bf16[256,256]{1,0:T(8,128)(2,1)} %constant.12.clone.element_hbm, ...), custom_call_target="tpu_custom_call" | custom-call | tf_op jit(solution)/shard_map/focus/pallas_call | solution.py:379
  31.1 1.3 %copy.10 = f32[4,4]{1,0:T(4,128)} copy(f32[4,4]{1,0:T(4,128)} %bitcast.4) | data formatting | bytes 128

commit v4 on v3

--- a/solution.py
+++ b/solution.py
@@ -161,7 +161,7 @@
     odd_loads = pieces(8, odd_hbm, odd_ref, 2)
     filter_loads = pieces(10, element_hbm, element_ref, 1) + pieces(11, depth_hbm, depth_ref, 4)
     column_loads = pieces(15, column_hbm, column_ref, 1)
-    for copy in raw_loads + even_loads[0]:
+    for copy in raw_loads + even_loads[0] + even_loads[1]:
         copy.start()
 
     barrier = pltpu.get_barrier_semaphore()
@@ -269,8 +269,6 @@
         keep(out[:half_rows], ODD[0], index)
         keep(out[half_rows:], ODD[1], 1 - index)
 
-    for copy in even_loads[1]:
-        copy.start()
     for copy in raw_loads + even_loads[0] + even_loads[1]:
         copy.wait()
     for copy in odd_loads + filter_loads + column_loads:
@@ -330,41 +328,34 @@
         partial[tile] = (both[:IZ, columns] + both[IZ:, columns]) * scale
 
     pl.semaphore_wait(barrier, len(PLANE) + len(PENCIL))
-    copies = []
     for index, step in enumerate(PLANE):
         copy = pltpu.make_async_remote_copy(
             src_ref=partial.at[(y + step[0]) & 3],
             dst_ref=inbox.at[index],
-            send_sem=send.at[index],
-            recv_sem=recv.at[index],
+            send_sem=send,
+            recv_sem=recv,
             device_id=plane_device(*step),
             device_id_type=MESH,
         )
         copy.start()
-        copies.append(copy)
-    total = partial[y]
-    for index in reversed(range(len(PLANE))):
-        copies[index].wait_recv()
-        total = total + inbox[index]
+    pltpu.make_async_copy(inbox, inbox, recv).wait()
+    total = partial[y] + jnp.sum(inbox[...], axis=0)
     middle[...] = total
-    copies2 = []
     for index, step in enumerate(PENCIL):
         copy = pltpu.make_async_remote_copy(
             src_ref=middle,
             dst_ref=inbox2.at[index],
-            send_sem=send2.at[index],
-            recv_sem=recv2.at[index],
+            send_sem=send2,
+            recv_sem=recv2,
             device_id=pencil_device(*step),
             device_id_type=MESH,
         )
         copy.start()
-        copies2.append(copy)
-    for index in reversed(range(len(PENCIL))):
-        copies2[index].wait_recv()
-        total = total + inbox2[index]
+    pltpu.make_async_copy(inbox2, inbox2, recv2).wait()
+    total = total + jnp.sum(inbox2[...], axis=0)
     out_ref[...] = pltpu.roll(total, (128 - (x_chip * 32 + z_chip * 4)) & 127, 1)
-    for copy in copies + copies2:
-        copy.wait_send()
+    pltpu.make_async_copy(inbox, inbox, send).wait()
+    pltpu.make_async_copy(inbox2, inbox2, send2).wait()
 
 
 def focus(raw, band_bins, probe_index):
@@ -395,10 +386,10 @@
             pltpu.VMEM((15, *tile), jnp.float32),
             pltpu.VMEM(tile, jnp.float32),
             pltpu.VMEM((15, *tile), jnp.float32),
-            pltpu.SemaphoreType.DMA((15,)),
-            pltpu.SemaphoreType.DMA((15,)),
-            pltpu.SemaphoreType.DMA((15,)),
-            pltpu.SemaphoreType.DMA((15,)),
+            pltpu.SemaphoreType.DMA,
+            pltpu.SemaphoreType.DMA,
+            pltpu.SemaphoreType.DMA,
+            pltpu.SemaphoreType.DMA,
         ],
         compiler_params=pltpu.CompilerParams(
             collective_id=0, has_side_effects=True, vmem_limit_bytes=63 * 1024 * 1024

time: 32.5 us -> 31.9 us (0.982)
  Pallas kernels: 31.1 us -> 30.5 us
    pallas_call x1, Pallas kernels: 31.1 us -> 30.5 us  [focus(): pl.pallas_call(focus_kernel, out_shape=jax.ShapeDtypeStruct(tile, jnp.flo...]
where the time goes in v4:
time: 31.9 us; the launch traced here: 31.8 us
  Pallas kernels  30.5 us (96%)
  local copies, waits for them, and re-layouts  1.26 us (4%)
    pallas_call x1, Pallas kernels, focus(): pl.pallas_call(focus_kernel, out_shape=jax.ShapeDtypeStruct(tile, jnp.flo...  30.5 us
    unnamed x1, local copies, waits for them, and re-layouts  1.26 us

profile of v4, /device:TPU:1, one launch (start us, length us, event | category | flops | bytes accessed | tf_op | source)
XLA Modules:
  0.0 31.8 jit_solution(5526331233116993928)
XLA Ops:
  0.0 30.5 %focus.1 = f32[4,128]{1,0:T(4,128)} custom-call(s32[2]{0:T(128)} %probe_ref.1, s32[1,1024]{1,0:T(1,128)} %bitcast.5, bf16[256,4096]{1,0:T(8,128)(2,1)} %bitcast.3, bf16[2,480,1024]{2,1,0:T(8,128)(2,1)} %constant.10.clone.even_hbm, bf16[480,2048]{1,0:T(8,128)(2,1)} %constant.11.clone.odd_hbm, bf16[256,256]{1,0:T(8,128)(2,1)} %constant.12.clone.element_hbm, ...), custom_call_target="tpu_custom_call" | custom-call | tf_op jit(solution)/shard_map/focus/pallas_call | solution.py:370
  30.5 1.3 %copy.10 = f32[4,4]{1,0:T(4,128)} copy(f32[4,4]{1,0:T(4,128)} %bitcast.4) | data formatting | bytes 128

commit v5 on v4

--- a/solution.py
+++ b/solution.py
@@ -320,8 +320,10 @@
     both = jnp.concatenate([image[tile] for tile in range(TILES)], axis=1)
     is_first = lax.broadcasted_iota(jnp.int32, (POS_HERE * IZ, IX), 0) < IZ
     turn = jnp.where(is_first, probe_ref[0] + probe_anchor, probe_ref[1] + probe_anchor)
-    for bit in range(7):
-        both = jnp.where(((turn >> bit) & 1) == 1, pltpu.roll(both, 4 << bit, 1), both)
+    for bit in range(0, 8, 2):
+        two = (turn >> bit) & 3
+        once, twice, thrice = [pltpu.roll(both, (4 * i << bit) % IX, 1) for i in (1, 2, 3)]
+        both = jnp.where(two == 0, both, jnp.where(two == 1, once, jnp.where(two == 2, twice, thrice)))
     scale = 1.0 / math.sqrt(float(NT * NE**3 * NF * 4))
     for tile in range(TILES):
         columns = slice(tile * 128, (tile + 1) * 128)

time: 31.9 us -> 31.8 us (level)
  no operation moved by 1% of the time
where the time goes in v5:
time: 31.8 us; the launch traced here: 31.6 us
  Pallas kernels  30.4 us (96%)
  local copies, waits for them, and re-layouts  1.26 us (4%)
    pallas_call x1, Pallas kernels, focus(): pl.pallas_call(focus_kernel, out_shape=jax.ShapeDtypeStruct(tile, jnp.flo...  30.4 us
    unnamed x1, local copies, waits for them, and re-layouts  1.26 us

profile of v5, /device:TPU:1, one launch (start us, length us, event | category | flops | bytes accessed | tf_op | source)
XLA Modules:
  0.0 31.6 jit_solution(5244285470652019324)
XLA Ops:
  0.0 30.4 %focus.1 = f32[4,128]{1,0:T(4,128)} custom-call(s32[2]{0:T(128)} %probe_ref.1, s32[1,1024]{1,0:T(1,128)} %bitcast.5, bf16[256,4096]{1,0:T(8,128)(2,1)} %bitcast.3, bf16[2,480,1024]{2,1,0:T(8,128)(2,1)} %constant.10.clone.even_hbm, bf16[480,2048]{1,0:T(8,128)(2,1)} %constant.11.clone.odd_hbm, bf16[256,256]{1,0:T(8,128)(2,1)} %constant.12.clone.element_hbm, ...), custom_call_target="tpu_custom_call" | custom-call | tf_op jit(solution)/shard_map/focus/pallas_call | solution.py:372
  30.4 1.3 %copy.10 = f32[4,4]{1,0:T(4,128)} copy(f32[4,4]{1,0:T(4,128)} %bitcast.4) | data formatting | bytes 128

commit v6 on v5

--- a/solution.py
+++ b/solution.py
@@ -163,12 +163,6 @@
     column_loads = pieces(15, column_hbm, column_ref, 1)
     for copy in raw_loads + even_loads[0] + even_loads[1]:
         copy.start()
-
-    barrier = pltpu.get_barrier_semaphore()
-    for step in PLANE:
-        pl.semaphore_signal(barrier, inc=1, device_id=plane_device(*step), device_id_type=MESH)
-    for step in PENCIL:
-        pl.semaphore_signal(barrier, inc=1, device_id=pencil_device(*step), device_id_type=MESH)
 
     bins = bins_ref[...] - LOWEST
     centre = (bins * 3277) >> 16
@@ -277,6 +271,11 @@
     for q in range(1, 4):
         negative[:, q * QUARTER : (q + 1) * QUARTER] = -raw_ref[:, q * QUARTER : (q + 1) * QUARTER]
     even_bins(1)
+    barrier = pltpu.get_barrier_semaphore()
+    for step in PLANE:
+        pl.semaphore_signal(barrier, inc=1, device_id=plane_device(*step), device_id_type=MESH)
+    for step in PENCIL:
+        pl.semaphore_signal(barrier, inc=1, device_id=pencil_device(*step), device_id_type=MESH)
     for copy in odd_loads + filter_loads + column_loads:
         copy.wait()
     filtered(0, 0)

time: 31.8 us -> 32.1 us (level)
  no operation moved by 1% of the time
where the time goes in v6:
time: 32.1 us; the launch traced here: 31.9 us
  Pallas kernels  30.7 us (96%)
  local copies, waits for them, and re-layouts  1.26 us (4%)
    pallas_call x1, Pallas kernels, focus(): pl.pallas_call(focus_kernel, out_shape=jax.ShapeDtypeStruct(tile, jnp.flo...  30.7 us
    unnamed x1, local copies, waits for them, and re-layouts  1.26 us

profile of v6, /device:TPU:1, one launch (start us, length us, event | category | flops | bytes accessed | tf_op | source)
XLA Modules:
  0.0 31.9 jit_solution(18106896004754017541)
XLA Ops:
  0.0 30.7 %focus.1 = f32[4,128]{1,0:T(4,128)} custom-call(s32[2]{0:T(128)} %probe_ref.1, s32[1,1024]{1,0:T(1,128)} %bitcast.5, bf16[256,4096]{1,0:T(8,128)(2,1)} %bitcast.3, bf16[2,480,1024]{2,1,0:T(8,128)(2,1)} %constant.10.clone.even_hbm, bf16[480,2048]{1,0:T(8,128)(2,1)} %constant.11.clone.odd_hbm, bf16[256,256]{1,0:T(8,128)(2,1)} %constant.12.clone.element_hbm, ...), custom_call_target="tpu_custom_call" | custom-call | tf_op jit(solution)/shard_map/focus/pallas_call | solution.py:371
  30.7 1.3 %copy.10 = f32[4,4]{1,0:T(4,128)} copy(f32[4,4]{1,0:T(4,128)} %bitcast.4) | data formatting | bytes 128
